TPU v7x, 512 devices: a whole 4x8x8 slice. The times are simulated.
512 devices in a mesh: grp: 8 (over y), row: 8 (over z), col: 8 (over x, core).
Axes of the slice: x: 4, y: 8, z: 8, core: 2. Of those that a mesh axis runs over, the one named last changes fastest.
Arguments:
- new_rows: bfloat16 [768, 16, 8192], P(('grp', 'col'), None, 'row'), may hold values from -6 to 6
- query_weight: bfloat16 [8192, 8192], P('row', 'col')
- key_weight: bfloat16 [8192, 1024], P('row', 'col')
- value_weight: bfloat16 [8192, 1024], P('row', 'col'), may hold values from -0.0625 to 0.0625
- cache_keys: bfloat16 [768, 512, 1024], P(('grp', 'row'), None, 'col'), may hold values from -6 to 6
- cache_values: bfloat16 [768, 512, 1024], P(('grp', 'row'), None, 'col'), may hold values from -6 to 6
- region_agents: int32 [768], replicated, may hold values from 0 to 767, as said below
- new_counts: int32 [768], replicated, may hold values from 4 to 16, as said below
- cache_lengths: int32 [768], replicated, may hold values from 1 to 512, as said below
Outputs:
- attended: bfloat16 [768, 16, 8192], P(('grp', 'col'), 'row')
Inputs may be any that keep to these rules, and one draw needn't show every extreme that they name: `region_agents`: A permutation of the 768 agents. Rows i with equal i // 12 form one region; agent a is served by group a // 96. Every region holds at most 3 agents served by one group, and exactly 3 of some group. `new_counts`: some agent has 16 new tokens. `cache_lengths`: some agent has 512 cached positions.
All inputs are finite; a program needn't handle non-finite values.
Results may differ from a plain program's by a relative error of at most 0.025.
Values may be sent and summed in bfloat16 or wider, within the bound.
A program may use at most 64 MiB of HBM per device.

v0:
```python
import jax
import jax.numpy as jnp
from jax import lax
from jax.sharding import PartitionSpec as P

HEAD_DIM = 128
rotary_base = 500000.0
floor_score = -1e30


def rotate_pairs(values, positions):
    half_dim = values.shape[-1] // 2
    exponent = jnp.arange(half_dim, dtype=jnp.float32) * (2.0 / values.shape[-1])
    frequency = rotary_base ** (-exponent)
    angles = positions.astype(jnp.float32)[..., None, None] * frequency
    cosine = jnp.cos(angles)
    sine_part = jnp.sin(angles)
    first_half = values[..., :half_dim]
    second = values[..., half_dim:]
    return jnp.concatenate(
        [first_half * cosine - second * sine_part, second * cosine + first_half * sine_part],
        axis=-1,
    )


def local(
    new_rows,
    query_weight,
    key_weight,
    value_weight,
    cache_keys,
    cache_values,
    region_agents,
    new_counts,
    cache_lengths,
):
    groups = lax.axis_size("grp")
    grid_rows = lax.axis_size("row")
    grid_cols = lax.axis_size("col")
    group_index = lax.axis_index("grp")
    row_index = lax.axis_index("row")
    col_index = lax.axis_index("col")
    agents_total = region_agents.shape[0]
    per_group = agents_total // groups
    per_region = new_rows.shape[0]
    regions = groups * grid_cols
    capacity = max(2, 2 * per_region // groups)
    slot_count = new_rows.shape[1]
    feature_width = new_rows.shape[2]
    slot_width = slot_count // grid_cols
    served_by = region_agents // per_group
    grouped = served_by.reshape(regions, per_region)
    earlier = jnp.arange(per_region)[:, None] > jnp.arange(per_region)[None, :]
    same_group = grouped[:, :, None] == grouped[:, None, :]
    bucket = jnp.sum((same_group & earlier[None, :, :]).astype(jnp.int32), axis=2).reshape(
        agents_total
    )
    slot_of_agent = jnp.argsort(region_agents)
    my_region = group_index * grid_cols + col_index
    mine_group = lax.dynamic_slice_in_dim(served_by, my_region * per_region, per_region)
    mine_bucket = lax.dynamic_slice_in_dim(bucket, my_region * per_region, per_region)
    choose = (
        (mine_group[None, None, :] == jnp.arange(groups)[:, None, None])
        & (mine_bucket[None, None, :] == jnp.arange(capacity)[None, :, None])
    ).astype(jnp.bfloat16)
    pieces = new_rows.reshape(per_region, grid_cols, slot_width, feature_width)
    outgoing = jnp.einsum(
        "gkj,jcsd->gcksd", choose, pieces, preferred_element_type=jnp.float32
    ).astype(jnp.bfloat16)
    arrived = lax.all_to_all(
        outgoing.reshape(regions, capacity, slot_width, feature_width),
        ("grp", "col"),
        split_axis=0,
        concat_axis=0,
        tiled=True,
    )
    my_slots = lax.dynamic_slice_in_dim(slot_of_agent, group_index * per_group, per_group)
    source_row = my_slots // per_region * capacity + jnp.take(bucket, my_slots)
    landed = jnp.take(
        arrived.reshape(regions * capacity, slot_width, feature_width), source_row, axis=0
    )
    tokens = lax.all_gather(landed, "col", axis=1, tiled=True)
    agents_here = cache_keys.shape[0]
    picked = tokens.reshape(lax.axis_size("row") * agents_here * slot_count, feature_width)
    query_part = jnp.dot(picked, query_weight, preferred_element_type=jnp.float32)
    key_part = jnp.dot(picked, key_weight, preferred_element_type=jnp.float32)
    value_part = jnp.dot(picked, value_weight, preferred_element_type=jnp.float32)
    summed = lax.psum_scatter(
        jnp.concatenate([query_part, key_part, value_part], axis=1)
        .reshape(lax.axis_size("row") * agents_here, slot_count, -1)
        .astype(jnp.bfloat16),
        "row",
        scatter_dimension=0,
        tiled=True,
    ).astype(jnp.float32)
    local_agents = (
        group_index * per_group + row_index * agents_here + jnp.arange(agents_here, dtype=jnp.int32)
    )
    lengths_now = jnp.take(cache_lengths, local_agents)
    counts_now = jnp.take(new_counts, local_agents)
    positions = lengths_now[:, None] + jnp.arange(slot_count, dtype=jnp.int32)[None, :]
    query_width = query_weight.shape[1]
    key_width = key_weight.shape[1]
    heads_here = query_width // HEAD_DIM
    kv_here = key_width // HEAD_DIM
    group_ratio = heads_here // kv_here
    queries = rotate_pairs(
        summed[:, :, :query_width].reshape(agents_here, slot_count, heads_here, HEAD_DIM), positions
    ).astype(jnp.bfloat16)
    fresh_keys = rotate_pairs(
        summed[:, :, query_width : query_width + key_width].reshape(
            agents_here, slot_count, kv_here, HEAD_DIM
        ),
        positions,
    ).astype(jnp.bfloat16)
    fresh_values = (
        summed[:, :, query_width + key_width :]
        .reshape(agents_here, slot_count, kv_here, HEAD_DIM)
        .astype(jnp.bfloat16)
    )
    query_rows = (
        queries.reshape(agents_here, slot_count, kv_here, group_ratio, HEAD_DIM)
        .transpose(0, 2, 3, 1, 4)
        .reshape(agents_here, kv_here, group_ratio * slot_count, HEAD_DIM)
    )
    cache_span = cache_keys.shape[1]
    stored_keys = cache_keys.reshape(agents_here, cache_span, kv_here, HEAD_DIM)
    stored_values = cache_values.reshape(agents_here, cache_span, kv_here, HEAD_DIM)
    score_scale = HEAD_DIM ** (-0.5)
    slot_of_row = jnp.arange(group_ratio * slot_count, dtype=jnp.int32) % slot_count
    fresh_index = jnp.arange(slot_count, dtype=jnp.int32)
    new_allowed = (
        (fresh_index[None, :] <= slot_of_row[:, None])[None, :, :]
        & (fresh_index[None, None, :] < counts_now[:, None, None])
    )[:, None, :, :]
    new_scores = (
        jnp.einsum("akrd,atkd->akrt", query_rows, fresh_keys, preferred_element_type=jnp.float32)
        * score_scale
    )
    cache_scores = (
        jnp.einsum("akrd,apkd->akrp", query_rows, stored_keys, preferred_element_type=jnp.float32)
        * score_scale
    )
    cache_allowed = (jnp.arange(cache_span, dtype=jnp.int32)[None, :] < lengths_now[:, None])[
        :, None, None, :
    ]
    cache_masked = jnp.where(cache_allowed, cache_scores, floor_score)
    new_masked = jnp.where(new_allowed, new_scores, floor_score)
    row_max = jnp.maximum(jnp.max(cache_masked, axis=3), jnp.max(new_masked, axis=3))
    cache_weights = jnp.where(cache_allowed, jnp.exp(cache_masked - row_max[..., None]), 0.0)
    new_weights = jnp.where(new_allowed, jnp.exp(new_masked - row_max[..., None]), 0.0)
    denominator = jnp.sum(cache_weights, axis=3) + jnp.sum(new_weights, axis=3)
    weighted = jnp.einsum(
        "akrp,apkd->akrd",
        cache_weights.astype(jnp.bfloat16),
        stored_values,
        preferred_element_type=jnp.float32,
    )
    weighted = weighted + jnp.einsum(
        "akrp,apkd->akrd",
        new_weights.astype(jnp.bfloat16),
        fresh_values,
        preferred_element_type=jnp.float32,
    )
    result = (
        (weighted / denominator[..., None])
        .reshape(agents_here, kv_here, group_ratio, slot_count, HEAD_DIM)
        .transpose(0, 3, 1, 2, 4)
        .reshape(agents_here, slot_count, query_width)
    )
    valid_slot = jnp.arange(slot_count, dtype=jnp.int32)[None, :] < counts_now[:, None]
    result = jnp.where(valid_slot[:, :, None], result, 0.0).astype(jnp.bfloat16)
    regrouped = lax.all_to_all(result, "row", split_axis=1, concat_axis=0, tiled=True)
    slot_share = slot_count // grid_rows
    choose_back = (
        jnp.arange(regions * capacity, dtype=jnp.int32)[:, None] == source_row[None, :]
    ).astype(jnp.bfloat16)
    returning = jnp.einsum(
        "qt,tsf->qsf", choose_back, regrouped, preferred_element_type=jnp.float32
    ).astype(jnp.bfloat16)
    incoming = lax.all_to_all(
        returning.reshape(regions, capacity, slot_share, query_width),
        ("grp", "col"),
        split_axis=0,
        concat_axis=0,
        tiled=True,
    ).reshape(groups, grid_cols, capacity, slot_share, query_width)
    select_back = (
        (mine_group[:, None, None] == jnp.arange(groups)[None, :, None])
        & (mine_bucket[:, None, None] == jnp.arange(capacity)[None, None, :])
    ).astype(jnp.bfloat16)
    finished = jnp.einsum(
        "jgk,gcksf->jscf", select_back, incoming, preferred_element_type=jnp.float32
    ).astype(jnp.bfloat16)
    return finished.reshape(per_region, slot_share, grid_cols * query_width)


def solution(mesh):
    placed = (
        P(("grp", "col"), None, "row"),
        P("row", "col"),
        P("row", "col"),
        P("row", "col"),
        P(("grp", "row"), None, "col"),
        P(("grp", "row"), None, "col"),
        P(),
        P(),
        P(),
    )
    return jax.shard_map(
        local, mesh=mesh, in_specs=placed, out_specs=P(("grp", "col"), "row", None), check_vma=False
    )
```

profile of v0, /device:TPU:1, one launch (start us, length us, event | category | flops | bytes accessed | tf_op | source)
XLA Modules:
  0.0 230.3 jit_solution(6798773412891268803)
XLA Ops:
  6.5 0.8 add_select_fusion
  8.1 1.2 copy.95
  10.1 1.7 copy.77
  11.8 11.6 %all-to-all-start = ((bf16[64,3,2,1024]{3,2,1,0:T(2,128)(2,1)}), bf16[64,3,2,1024]{3,2,1,0:T(2,128)(2,1)S(1)}, u32[]{:S(2)}, u32[]{:S(2)}) async-start(bf16[64,3,2,1024]{3,2,1,0:T(2,128)(2,1)} %copy.77), calls=%async_computation | async-start | bytes 1572864 | tf_op jit(solution)/shard_map/all_to_all | solution.py:70
  23.5 4.4 %sort.17 = (s32[768]{0:T(1024)}, s32[768]{0:T(1024)S(1)}) sort(s32[768]{0:T(1024)S(1)} %copy-done.7, s32[768]{0:T(1024)S(1)} %iota.103), dimensions={0}, to_apply=%region_0.1 | sort | flops 7680 | bytes 12288 | tf_op jit(solution)/shard_map/jit(argsort)/sort | solution.py:58
  27.9 1.0 gather_fusion
  29.0 17.1 %all-to-all-done = bf16[64,3,2,1024]{3,2,1,0:T(2,128)(2,1)S(1)} async-done(((bf16[64,3,2,1024]{3,2,1,0:T(2,128)(2,1)}), bf16[64,3,2,1024]{3,2,1,0:T(2,128)(2,1)S(1)}, u32[]{:S(2)}, u32[]{:S(2)}) %all-to-all-start) | async-done | bytes 786464 | tf_op jit(solution)/shard_map/all_to_all | solution.py:70
  46.2 1.4 gather_fusion.1
  49.1 33.5 %all-gather.2.cloned.1.call-done = bf16[96,16,1024]{2,0,1:T(8,128)(2,1)} async-done(((bf16[96,2,1024]{2,0,1:T(8,128)(2,1)}), bf16[96,16,1024]{2,0,1:T(8,128)(2,1)}) %all-gather.2.cloned.1.call-update) | async-done | bytes 3145744 | tf_op jit(solution)/shard_map/all_gather | solution.py:82
  82.6 3.6 %copy.79 = bf16[96,16,1024]{2,1,0:T(8,128)(2,1)S(1)} copy(bf16[96,16,1024]{2,0,1:T(8,128)(2,1)} %all-gather.2.cloned.1.call-done) | data formatting | bytes 6291456 | tf_op jit(solution)/shard_map/all_gather | solution.py:82
  86.2 3.8 %convolution_convert_fusion = bf16[1536,1024]{0,1:T(8,128)(2,1)S(1)} fusion(bf16[1536,1024]{1,0:T(8,128)(2,1)S(1)} %bitcast.78, bf16[1024,1024]{1,0:T(8,128)(2,1)S(1)} %copy-done), kind=kOutput, calls=%fused_computation.5 | convolution fusion | flops 3222798336 | bytes 8388608 | tf_op jit(solution)/shard_map/dot_general | solution.py:85
  90.1 1.2 convolution_convert_fusion.1
  91.3 1.2 convolution_convert_fusion.2
  92.5 2.1 pad_maximum_fusion
  94.5 6.3 %copy.80 = bf16[1536,1280]{1,0:T(8,128)(2,1)} copy(bf16[1536,1280]{0,1:T(8,128)(2,1)} %pad_maximum_fusion) | data formatting | bytes 7864320 | tf_op jit(solution)/shard_map/concatenate | solution.py:89
  103.5 53.5 %reduce-scatter.2.cloned.1.call-done = bf16[12,16,1280]{2,1,0:T(8,128)(2,1)} async-done(((bf16[96,16,1280]{2,1,0:T(8,128)(2,1)}), bf16[12,16,1280]{2,1,0:T(8,128)(2,1)}) %reduce-scatter.2.cloned.1.call-update) | async-done | bytes 491536 | tf_op jit(solution)/shard_map/reduce_scatter | solution.py:88
  157.0 1.1 slice.37
  161.1 1.0 fusion.1
  162.2 1.1 fusion.3
  164.6 19.7 %all_to_all.28 = bf16[12,16,1024]{2,0,1:T(8,128)(2,1)S(1)} all-to-all(bf16[12,16,1024]{2,0,1:T(8,128)(2,1)S(1)} %copy.84), channel_id=1, replica_groups=mesh['grp'=8,'row'=8,'col'=8] {'row'}, dimensions={1} | all-to-all | bytes 786432 | tf_op jit(solution)/shard_map/all_to_all | solution.py:173
  185.1 1.7 copy.88
  186.7 12.2 %all-to-all-start.2 = ((bf16[64,3,2,1024]{3,2,1,0:T(2,128)(2,1)}), bf16[64,3,2,1024]{3,2,1,0:T(2,128)(2,1)S(1)}, u32[]{:S(2)}, u32[]{:S(2)}) async-start(bf16[64,3,2,1024]{3,2,1,0:T(2,128)(2,1)} %bitcast.24), calls=%async_computation.3 | async-start | bytes 1572864 | tf_op jit(solution)/shard_map/all_to_all | solution.py:181
  199.0 22.7 %all-to-all-done.2 = bf16[64,3,2,1024]{3,2,1,0:T(2,128)(2,1)S(1)} async-done(((bf16[64,3,2,1024]{3,2,1,0:T(2,128)(2,1)}), bf16[64,3,2,1024]{3,2,1,0:T(2,128)(2,1)S(1)}, u32[]{:S(2)}, u32[]{:S(2)}) %all-to-all-start.2) | async-done | bytes 786464 | tf_op jit(solution)/shard_map/all_to_all | solution.py:181
  222.5 1.0 reshape.419
  (77 shorter events, 11.7 us)
Async XLA Ops:
  6.5 79.7 %copy-start = (bf16[1024,1024]{1,0:T(8,128)(2,1)S(1)}, bf16[1024,1024]{1,0:T(8,128)(2,1)}, u32[]{:S(2)}) copy-start(bf16[1024,1024]{1,0:T(8,128)(2,1)} %param.12) | copy-start | bytes 6291460
  9.3 14.2 %copy-start.7 = (s32[768]{0:T(1024)S(1)}, s32[768]{0:T(1024)}, u32[]{:S(2)}) copy-start(s32[768]{0:T(1024)} %param.17) | copy-start | bytes 9220
  11.8 34.4 %all-to-all-start = ((bf16[64,3,2,1024]{3,2,1,0:T(2,128)(2,1)}), bf16[64,3,2,1024]{3,2,1,0:T(2,128)(2,1)S(1)}, u32[]{:S(2)}, u32[]{:S(2)}) async-start(bf16[64,3,2,1024]{3,2,1,0:T(2,128)(2,1)} %copy.77), calls=%async_computation | async-start | bytes 1572864 | tf_op jit(solution)/shard_map/all_to_all | solution.py:70
  23.4 59.2 %all-gather.2.cloned.1.call-start = ((), (), s32[]{:S(2)}) async-start(), calls=%async_computation.4 | async-start | bytes 3538944 | tf_op jit(solution)/shard_map/all_gather | solution.py:82
  48.8 108.1 %reduce-scatter.2.cloned.1.call-start = ((), (), s32[]{:S(2)}) async-start(), calls=%async_computation.5 | async-start | bytes 4423680 | tf_op jit(solution)/shard_map/reduce_scatter | solution.py:88
  86.2 3.8 %copy-start.5 = (bf16[1024,128]{1,0:T(8,128)(2,1)S(1)}, bf16[1024,128]{1,0:T(8,128)(2,1)}, u32[]{:S(2)}) copy-start(bf16[1024,128]{1,0:T(8,128)(2,1)} %param.14) | copy-start | bytes 786436
  90.1 1.2 copy-start.6
  100.8 0.7 copy-start.1
  100.8 1.3 copy-start.2
  157.0 1.6 copy-start.3
  158.5 1.4 copy-start.4
  160.6 1.5 copy-start.8
  186.7 34.9 %all-to-all-start.2 = ((bf16[64,3,2,1024]{3,2,1,0:T(2,128)(2,1)}), bf16[64,3,2,1024]{3,2,1,0:T(2,128)(2,1)S(1)}, u32[]{:S(2)}, u32[]{:S(2)}) async-start(bf16[64,3,2,1024]{3,2,1,0:T(2,128)(2,1)} %bitcast.24), calls=%async_computation.3 | async-start | bytes 1572864 | tf_op jit(solution)/shard_map/all_to_all | solution.py:181
Sparse Core Ops, SparseCore 0:
  49.0 33.5 all-gather.1
  100.9 55.9 reduce-scatter.1
where the time goes:
time: 231 us; the launch traced here: 230 us
  waiting for transfers between devices  127 us (55%)
  local copies, waits for them, and re-layouts  24.5 us (11%)
  starting transfers between devices  24.1 us (10%)
  blocking collectives  19.7 us (9%)
  between operations  13.8 us (6%)
  other arithmetic  11.2 us (5%)
  matrix products  10.2 us (4%)
    reduce_scatter x1, waiting for transfers between devices, local(): lax.psum_scatter(jnp.concatenate([query_part, key_part, value_part], axis...  53.5 us
    all_gather x1, waiting for transfers between devices, local(): tokens = lax.all_gather(landed, 'col', axis=1, tiled=True)  33.5 us
    all_to_all x1, waiting for transfers between devices, local(): lax.all_to_all(returning.reshape(regions, capacity, slot_share, query_wid...  22.7 us
    all_to_all x1, blocking collectives, local(): lax.all_to_all(result, 'row', split_axis=1, concat_axis=0, tiled=True)  19.7 us
    all_to_all x1, waiting for transfers between devices, local(): lax.all_to_all(outgoing.reshape(regions, capacity, slot_width, feature_wi...  17.1 us
    all_to_all x1, starting transfers between devices, local(): lax.all_to_all(returning.reshape(regions, capacity, slot_share, query_wid...  12.2 us
    all_to_all x1, starting transfers between devices, local(): lax.all_to_all(outgoing.reshape(regions, capacity, slot_width, feature_wi...  11.6 us
    concatenate x1, local copies, waits for them, and re-layouts, local(): jnp.concatenate([query_part, key_part, value_part], axis=1)  6.26 us
  transfers between devices with their start and end apart: 4, of which 4 were waited for; matrix products, arithmetic and copies ran while one was open for 3% of the time, Pallas kernels for 0%

commit v1 on v0

--- a/solution.py
+++ b/solution.py
@@ -170,7 +170,12 @@
     )
     valid_slot = jnp.arange(slot_count, dtype=jnp.int32)[None, :] < counts_now[:, None]
     result = jnp.where(valid_slot[:, :, None], result, 0.0).astype(jnp.bfloat16)
-    regrouped = lax.all_to_all(result, "row", split_axis=1, concat_axis=0, tiled=True)
+    regrouped = jnp.concatenate(
+        lax.all_to_all(
+            jnp.stack(jnp.split(result, lax.axis_size("row"), axis=1), axis=0), "row", 0, 0
+        ),
+        axis=0,
+    )
     slot_share = slot_count // grid_rows
     choose_back = (
         jnp.arange(regions * capacity, dtype=jnp.int32)[:, None] == source_row[None, :]

time: 231 us -> 228 us (0.987)
  blocking collectives: 19.7 us -> 17.2 us
    all_to_all x1, blocking collectives: 19.7 us -> 17.2 us  [local(): lax.all_to_all(jnp.stack(jnp.split(result, lax.axis_size('row'), axis=1),...]
where the time goes in v1:
time: 228 us; the launch traced here: 227 us
  waiting for transfers between devices  127 us (56%)
  local copies, waits for them, and re-layouts  24.3 us (11%)
  starting transfers between devices  23.7 us (10%)
  blocking collectives  17.2 us (8%)
  between operations  13.9 us (6%)
  other arithmetic  11.2 us (5%)
  matrix products  10.2 us (4%)
    reduce_scatter x1, waiting for transfers between devices, local(): lax.psum_scatter(jnp.concatenate([query_part, key_part, value_part], axis...  53.5 us
    all_gather x1, waiting for transfers between devices, local(): tokens = lax.all_gather(landed, 'col', axis=1, tiled=True)  33.5 us
    all_to_all x1, waiting for transfers between devices, local(): lax.all_to_all(returning.reshape(regions, capacity, slot_share, query_wid...  22.7 us
    all_to_all x1, blocking collectives, local(): lax.all_to_all(jnp.stack(jnp.split(result, lax.axis_size('row'), axis=1),...  17.2 us
    all_to_all x1, waiting for transfers between devices, local(): lax.all_to_all(outgoing.reshape(regions, capacity, slot_width, feature_wi...  17.1 us
    all_to_all x1, starting transfers between devices, local(): lax.all_to_all(returning.reshape(regions, capacity, slot_share, query_wid...  11.8 us
    all_to_all x1, starting transfers between devices, local(): lax.all_to_all(outgoing.reshape(regions, capacity, slot_width, feature_wi...  11.6 us
    concatenate x1, local copies, waits for them, and re-layouts, local(): jnp.concatenate([query_part, key_part, value_part], axis=1)  6.26 us
  transfers between devices with their start and end apart: 4, of which 4 were waited for; matrix products, arithmetic and copies ran while one was open for 3% of the time, Pallas kernels for 0%

profile of v1, /device:TPU:1, one launch (start us, length us, event | category | flops | bytes accessed | tf_op | source)
XLA Modules:
  0.0 227.4 jit_solution(4361786990367807276)
XLA Ops:
  6.5 0.8 add_select_fusion
  8.1 1.2 copy.92
  10.1 1.7 copy.77
  11.8 11.6 %all-to-all-start = ((bf16[64,3,2,1024]{3,2,1,0:T(2,128)(2,1)}), bf16[64,3,2,1024]{3,2,1,0:T(2,128)(2,1)S(1)}, u32[]{:S(2)}, u32[]{:S(2)}) async-start(bf16[64,3,2,1024]{3,2,1,0:T(2,128)(2,1)} %copy.77), calls=%async_computation | async-start | bytes 1572864 | tf_op jit(solution)/shard_map/all_to_all | solution.py:70
  23.5 4.4 %sort.17 = (s32[768]{0:T(1024)}, s32[768]{0:T(1024)S(1)}) sort(s32[768]{0:T(1024)S(1)} %copy-done.7, s32[768]{0:T(1024)S(1)} %iota.103), dimensions={0}, to_apply=%region_0.1 | sort | flops 7680 | bytes 12288 | tf_op jit(solution)/shard_map/jit(argsort)/sort | solution.py:58
  27.9 1.0 gather_fusion
  29.0 17.1 %all-to-all-done = bf16[64,3,2,1024]{3,2,1,0:T(2,128)(2,1)S(1)} async-done(((bf16[64,3,2,1024]{3,2,1,0:T(2,128)(2,1)}), bf16[64,3,2,1024]{3,2,1,0:T(2,128)(2,1)S(1)}, u32[]{:S(2)}, u32[]{:S(2)}) %all-to-all-start) | async-done | bytes 786464 | tf_op jit(solution)/shard_map/all_to_all | solution.py:70
  46.2 1.4 gather_fusion.1
  49.1 33.5 %all-gather.2.cloned.1.call-done = bf16[96,16,1024]{2,0,1:T(8,128)(2,1)} async-done(((bf16[96,2,1024]{2,0,1:T(8,128)(2,1)}), bf16[96,16,1024]{2,0,1:T(8,128)(2,1)}) %all-gather.2.cloned.1.call-update) | async-done | bytes 3145744 | tf_op jit(solution)/shard_map/all_gather | solution.py:82
  82.6 3.6 %copy.79 = bf16[96,16,1024]{2,1,0:T(8,128)(2,1)S(1)} copy(bf16[96,16,1024]{2,0,1:T(8,128)(2,1)} %all-gather.2.cloned.1.call-done) | data formatting | bytes 6291456 | tf_op jit(solution)/shard_map/all_gather | solution.py:82
  86.2 3.8 %convolution_convert_fusion = bf16[1536,1024]{0,1:T(8,128)(2,1)S(1)} fusion(bf16[1536,1024]{1,0:T(8,128)(2,1)S(1)} %bitcast.106, bf16[1024,1024]{1,0:T(8,128)(2,1)S(1)} %copy-done), kind=kOutput, calls=%fused_computation.5 | convolution fusion | flops 3222798336 | bytes 8388608 | tf_op jit(solution)/shard_map/dot_general | solution.py:85
  90.1 1.2 convolution_convert_fusion.1
  91.3 1.2 convolution_convert_fusion.2
  92.5 2.1 pad_maximum_fusion
  94.5 6.3 %copy.80 = bf16[1536,1280]{1,0:T(8,128)(2,1)} copy(bf16[1536,1280]{0,1:T(8,128)(2,1)} %pad_maximum_fusion) | data formatting | bytes 7864320 | tf_op jit(solution)/shard_map/concatenate | solution.py:89
  103.5 53.5 %reduce-scatter.2.cloned.1.call-done = bf16[12,16,1280]{2,1,0:T(8,128)(2,1)} async-done(((bf16[96,16,1280]{2,1,0:T(8,128)(2,1)}), bf16[12,16,1280]{2,1,0:T(8,128)(2,1)}) %reduce-scatter.2.cloned.1.call-update) | async-done | bytes 491536 | tf_op jit(solution)/shard_map/reduce_scatter | solution.py:88
  157.0 1.1 slice.37
  161.1 1.0 fusion.1
  162.2 1.1 fusion.3
  164.8 17.2 %all_to_all.15 = bf16[8,12,2,1024]{3,2,1,0:T(2,128)(2,1)S(1)} all-to-all(bf16[8,12,2,1024]{3,2,1,0:T(2,128)(2,1)S(1)} %fusion.32), channel_id=1, replica_groups=mesh['grp'=8,'row'=8,'col'=8] {'row'}, dimensions={0} | all-to-all | bytes 786432 | tf_op jit(solution)/shard_map/all_to_all | solution.py:174
  182.4 1.7 copy.85
  184.1 11.8 %all-to-all-start.2 = ((bf16[64,3,2,1024]{3,2,1,0:T(2,128)(2,1)}), bf16[64,3,2,1024]{3,2,1,0:T(2,128)(2,1)S(1)}, u32[]{:S(2)}, u32[]{:S(2)}) async-start(bf16[64,3,2,1024]{3,2,1,0:T(2,128)(2,1)} %bitcast.29), calls=%async_computation.3 | async-start | bytes 1572864 | tf_op jit(solution)/shard_map/all_to_all | solution.py:186
  196.0 22.7 %all-to-all-done.2 = bf16[64,3,2,1024]{3,2,1,0:T(2,128)(2,1)S(1)} async-done(((bf16[64,3,2,1024]{3,2,1,0:T(2,128)(2,1)}), bf16[64,3,2,1024]{3,2,1,0:T(2,128)(2,1)S(1)}, u32[]{:S(2)}, u32[]{:S(2)}) %all-to-all-start.2) | async-done | bytes 786464 | tf_op jit(solution)/shard_map/all_to_all | solution.py:186
  219.5 1.0 reshape.423
  (83 shorter events, 11.5 us)
Async XLA Ops:
  6.5 79.7 %copy-start = (bf16[1024,1024]{1,0:T(8,128)(2,1)S(1)}, bf16[1024,1024]{1,0:T(8,128)(2,1)}, u32[]{:S(2)}) copy-start(bf16[1024,1024]{1,0:T(8,128)(2,1)} %param.12) | copy-start | bytes 6291460
  9.3 14.2 %copy-start.7 = (s32[768]{0:T(1024)S(1)}, s32[768]{0:T(1024)}, u32[]{:S(2)}) copy-start(s32[768]{0:T(1024)} %param.17) | copy-start | bytes 9220
  11.8 34.4 %all-to-all-start = ((bf16[64,3,2,1024]{3,2,1,0:T(2,128)(2,1)}), bf16[64,3,2,1024]{3,2,1,0:T(2,128)(2,1)S(1)}, u32[]{:S(2)}, u32[]{:S(2)}) async-start(bf16[64,3,2,1024]{3,2,1,0:T(2,128)(2,1)} %copy.77), calls=%async_computation | async-start | bytes 1572864 | tf_op jit(solution)/shard_map/all_to_all | solution.py:70
  23.4 59.2 %all-gather.2.cloned.1.call-start = ((), (), s32[]{:S(2)}) async-start(), calls=%async_computation.4 | async-start | bytes 3538944 | tf_op jit(solution)/shard_map/all_gather | solution.py:82
  48.8 108.1 %reduce-scatter.2.cloned.1.call-start = ((), (), s32[]{:S(2)}) async-start(), calls=%async_computation.5 | async-start | bytes 4423680 | tf_op jit(solution)/shard_map/reduce_scatter | solution.py:88
  86.2 3.8 %copy-start.5 = (bf16[1024,128]{1,0:T(8,128)(2,1)S(1)}, bf16[1024,128]{1,0:T(8,128)(2,1)}, u32[]{:S(2)}) copy-start(bf16[1024,128]{1,0:T(8,128)(2,1)} %param.14) | copy-start | bytes 786436
  90.1 1.2 copy-start.6
  100.8 0.7 copy-start.1
  100.8 1.3 copy-start.2
  157.0 1.6 copy-start.3
  158.5 1.4 copy-start.4
  160.6 1.5 copy-start.8
  184.1 34.6 %all-to-all-start.2 = ((bf16[64,3,2,1024]{3,2,1,0:T(2,128)(2,1)}), bf16[64,3,2,1024]{3,2,1,0:T(2,128)(2,1)S(1)}, u32[]{:S(2)}, u32[]{:S(2)}) async-start(bf16[64,3,2,1024]{3,2,1,0:T(2,128)(2,1)} %bitcast.29), calls=%async_computation.3 | async-start | bytes 1572864 | tf_op jit(solution)/shard_map/all_to_all | solution.py:186
Sparse Core Ops, SparseCore 0:
  49.0 33.5 all-gather.1
  100.9 55.9 reduce-scatter.1
